TPU v7x, 32 devices: a whole 2x2x4 slice. The times are simulated.
32 devices in a mesh: rows: 16 (over z, y, x), cols: 2 (over core).
Axes of the slice: x: 2, y: 2, z: 4, core: 2. Of those that a mesh axis runs over, the one named last changes fastest.
Arguments:
- features: float32 [16, 2048], P(None, ('rows', 'cols')), may hold values from -4 to 4
- targets: float32 [32, 2048], P(None, ('rows', 'cols')), may hold values from -6 to 6
- point_order: int32 [2048], P(('rows', 'cols')), may hold values from 0 to 2047, as said below
- lengthscale: float32 [16], replicated, may hold values from 1 to 1.8
- noise_var: float32 [32], replicated, may hold values from 0.1 to 1
Outputs:
- solution: float32 [32, 2048], P(None, ('rows', 'cols'))
- residual: float32 [32, 2048], P(None, ('rows', 'cols'))
Inputs may be any that keep to these rules, and one draw needn't show every extreme that they name: `point_order`: each aligned block of 128 entries, the k-th one, holds each of the numbers k * 128 to k * 128 + 127 exactly once.
All inputs are finite; a program needn't handle non-finite values.
Results may differ from a plain program's by a relative error of at most 0.0051.
Values may be sent and summed in bfloat16 or wider, within the bound.
A program may use at most 64 MiB of HBM per device.

v0:
```python
import math

import jax
import jax.numpy as jnp
from jax import lax
from jax.sharding import PartitionSpec as P

INNER = 3
OUTER = 2


def kernel_tile(col_feat, col_norm, row_feat, row_norm):
    inner_prod = jnp.dot(
        col_feat.T, row_feat, precision=lax.Precision.HIGHEST, preferred_element_type=jnp.float32
    )
    return jnp.exp(-0.5 * (col_norm[:, None] + row_norm[None, :] - 2.0 * inner_prod)).astype(
        jnp.bfloat16
    )


def apply_columns(running, portion, col_feat, col_norm, row_feat, row_norm):
    columns = portion.shape[1]
    sub_cols = math.gcd(columns, 512)

    def advance(which, summed):
        offset = which * sub_cols
        part_feat = lax.dynamic_slice_in_dim(col_feat, offset, sub_cols, 1)
        part_norm = lax.dynamic_slice_in_dim(col_norm, offset, sub_cols, 0)
        part_vec = lax.dynamic_slice_in_dim(portion, offset, sub_cols, 1)
        kern_tile = kernel_tile(part_feat, part_norm, row_feat, row_norm)
        return summed + jnp.dot(part_vec, kern_tile, preferred_element_type=jnp.float32)

    return lax.fori_loop(0, columns // sub_cols, advance, running)


def body(features, targets, point_order, lengthscale, noise_var):
    scaled = features / lengthscale[:, None]
    row_norms = jnp.sum(scaled * scaled, 0)
    block_feat, block_targ = (
        lax.all_gather(scaled, "cols", axis=1, tiled=True),
        lax.all_gather(targets, "cols", axis=1, tiled=True),
    )
    block_norms = jnp.sum(block_feat * block_feat, 0)
    block_first = lax.axis_index("rows") * block_feat.shape[1]
    residual = jnp.take(block_targ, point_order - block_first, axis=1)
    noise_col = noise_var[:, None]
    own_len = scaled.shape[1]
    col_feat = lax.all_gather(scaled, ("rows", "cols"), axis=1, tiled=True)
    col_norm = jnp.sum(col_feat * col_feat, 0)
    solution = jnp.zeros_like(residual)
    for outer_turn in range(OUTER):
        remains = lax.all_gather(residual, "cols", axis=1, tiled=True)
        res_norm = jnp.sum(remains * remains, 1)
        direction = remains
        correction = jnp.zeros_like(remains)
        for inner_turn in range(INNER):
            block_packed = direction.astype(jnp.bfloat16)
            blank_block = jnp.zeros(block_packed.shape, jnp.float32)
            applied = (
                apply_columns(
                    blank_block, block_packed, block_feat, block_norms, block_feat, block_norms
                )
                + noise_col * direction
            )
            curvature = jnp.sum(direction * applied, 1)
            step_len = res_norm / curvature
            correction = correction + step_len[:, None] * direction
            remains = remains - step_len[:, None] * applied
            if inner_turn + 1 < INNER:
                new_norm = jnp.sum(remains * remains, 1)
                direction = remains + (new_norm / res_norm)[:, None] * direction
                res_norm = new_norm
        correction = lax.dynamic_slice_in_dim(
            correction, lax.axis_index("cols") * own_len, own_len, 1
        )
        packed = correction.astype(jnp.bfloat16)
        blank = jnp.zeros((packed.shape[0], scaled.shape[1]), jnp.float32)
        applied = (
            apply_columns(
                blank,
                lax.all_gather(packed, ("rows", "cols"), axis=1, tiled=True),
                col_feat,
                col_norm,
                scaled,
                row_norms,
            )
            + noise_col * correction
        )
        cross_term, energy = lax.psum(
            (jnp.sum(residual * applied, 1), jnp.sum(applied * applied, 1)), ("rows", "cols")
        )
        damping_w = cross_term / (energy + 1e-06)
        solution = solution + damping_w[:, None] * correction
        residual = residual - damping_w[:, None] * applied
    return (solution, residual)


def solution(mesh):
    return jax.shard_map(
        body,
        mesh=mesh,
        in_specs=(
            P(None, ("rows", "cols")),
            P(None, ("rows", "cols")),
            P(("rows", "cols")),
            P(),
            P(),
        ),
        out_specs=(P(None, ("rows", "cols")), P(None, ("rows", "cols"))),
        check_vma=False,
    )
```

profile of v0, /device:TPU:0, one launch (start us, length us, event | category | flops | bytes accessed | tf_op | source)
XLA Modules:
  0.0 218.2 jit_solution(4122270469793558248)
XLA Ops:
  0.6 0.8 multiply_reduce_fusion.15
  1.4 1.9 all-gather.2
  3.5 0.3 fusion.19
  3.8 0.3 copy-done.2
  4.1 0.4 copy-done
  4.5 1.8 all-gather
  6.4 0.6 gather_fusion
  7.1 1.8 all-gather.1
  9.0 0.6 copy-done.1
  9.6 0.2 multiply_reduce_fusion.12
  9.8 0.2 multiply_reduce_fusion.11
  10.1 0.2 multiply_reduce_fusion.10
  10.4 0.2 multiply_reduce_fusion.9
  10.7 0.2 fusion.22
  11.0 43.8 %all-gather.3 = bf16[32,64,32]{1,2,0:T(8,128)(2,1)S(1)} all-gather(bf16[1,64,32]{1,2,0:T(8,128)(2,1)S(1)} %get-tuple-element.456), channel_id=1, replica_groups=mesh['rows'=16,'cols'=2] {'rows','cols'}, dimensions={0}, use_global_device_ids=true | all-gather | bytes 135168 | tf_op jit(solution)/shard_map/all_gather | solution.py:81
  54.9 0.3 reshape.85
  55.2 37.4 %all-gather.4 = f32[32,64,16]{1,2,0:T(8,128)S(1)} all-gather(f32[1,64,16]{1,2,0:T(8,128)S(1)} %bitcast.95), channel_id=1, replica_groups=mesh['rows'=16,'cols'=2] {'rows','cols'}, dimensions={0}, use_global_device_ids=true | all-gather | bytes 135168 | tf_op jit(solution)/shard_map/all_gather | solution.py:48
  92.8 2.3 %while.18 = (s32[]{:T(128)}, f32[32,64]{1,0:T(8,128)S(1)}, bf16[32,2048]{1,0:T(8,128)(2,1)S(1)}, f32[2048]{0:T(1024)S(1)}, f32[64]{0:T(128)S(1)}, /*index=5*/f32...) while((s32[]{:T(128)}, f32[32,64]{1,0:T(8,128)S(1)}, ...), condition=%wide.region_10.11_spmd.clone, body=%wide.region_9.10_spmd.clone.sunk | while | flops 8556551 | bytes 236209 | solution.py:33
  92.9 0.3 fusion.65
  93.3 0.1 convolution_add_fusion.10
  93.5 0.3 fusion.65
  93.8 0.1 convolution_add_fusion.10
  94.0 0.3 fusion.65
  94.4 0.1 convolution_add_fusion.10
  94.6 0.3 fusion.65
  94.9 0.1 convolution_add_fusion.10
  95.1 0.2 multiply_reduce_fusion.8
  95.3 37.0 %all-reduce.1 = (f32[32]{0:T(128)S(1)}, f32[32]{0:T(128)S(1)}) all-reduce(f32[32]{0:T(128)S(1)} %get-tuple-element.413, f32[32]{0:T(128)S(1)} %get-tuple-element.412), channel_id=1, replica_groups=mesh['rows'=16,'cols'=2] {'rows','cols'}, use_global_device_ids=true, to_apply=%region_12.13 | all-reduce | flops 64 | bytes 512 | tf_op jit(solution)/shard_map/psum | solution.py:89
  132.3 1.8 all-gather.5
  134.3 0.2 multiply_reduce_fusion.6
  134.5 0.2 multiply_reduce_fusion.5
  134.8 0.2 multiply_reduce_fusion.4
  135.1 0.2 multiply_reduce_fusion.3
  135.3 0.2 fusion.23
  135.7 42.1 %all-gather.6 = bf16[32,64,32]{1,2,0:T(8,128)(2,1)S(1)} all-gather(bf16[1,64,32]{1,2,0:T(8,128)(2,1)S(1)} %get-tuple-element.449), channel_id=1, replica_groups=mesh['rows'=16,'cols'=2] {'rows','cols'}, dimensions={0}, use_global_device_ids=true | all-gather | bytes 135168 | tf_op jit(solution)/shard_map/all_gather | solution.py:81
  177.9 0.3 reshape.91
  178.2 2.3 %while.19 = (s32[]{:T(128)}, f32[32,64]{1,0:T(8,128)S(1)}, bf16[32,2048]{1,0:T(8,128)(2,1)S(1)}, f32[2048]{0:T(1024)S(1)}, f32[64]{0:T(128)S(1)}, /*index=5*/f32...) while((s32[]{:T(128)}, f32[32,64]{1,0:T(8,128)S(1)}, ...), condition=%wide.region_22.23_spmd.clone, body=%wide.region_21.22_spmd.clone.sunk | while | flops 8556551 | bytes 236209 | solution.py:33
  178.3 0.3 fusion.70
  178.6 0.1 convolution_add_fusion.11
  178.8 0.3 fusion.70
  179.2 0.1 convolution_add_fusion.11
  179.4 0.3 fusion.70
  179.7 0.1 convolution_add_fusion.11
  179.9 0.3 fusion.70
  180.3 0.1 convolution_add_fusion.11
  180.4 0.2 multiply_reduce_fusion.1
  180.6 36.9 %all-reduce = (f32[32]{0:T(128)S(1)}, f32[32]{0:T(128)S(1)}) all-reduce(f32[32]{0:T(128)S(1)} %get-tuple-element.409, f32[32]{0:T(128)S(1)} %get-tuple-element.408), channel_id=1, replica_groups=mesh['rows'=16,'cols'=2] {'rows','cols'}, use_global_device_ids=true, to_apply=%region_24.25 | all-reduce | flops 64 | bytes 512 | tf_op jit(solution)/shard_map/psum | solution.py:89
  217.5 0.7 multiply_subtract_fusion
  (49 shorter events, 2.2 us)
Async XLA Ops:
  3.5 0.7 copy-start.2
  3.8 0.7 copy-start
  8.9 0.7 copy-start.1
where the time goes:
time: 219 us; the launch traced here: 218 us
  blocking collectives  204 us (93%)
  matrix products  5.49 us (3%)
  local copies, waits for them, and re-layouts  3.91 us (2%)
  other arithmetic  3.3 us (2%)
    all_gather x2, blocking collectives, body(): lax.all_gather(packed, ('rows', 'cols'), axis=1, tiled=True)  85.9 us
    psum x2, blocking collectives, body(): lax.psum((jnp.sum(residual * applied, 1), jnp.sum(applied * applied, 1)),...  73.9 us
    all_gather x1, blocking collectives, body(): col_feat = lax.all_gather(scaled, ('rows', 'cols'), axis=1, tiled=True)  37.4 us

commit v1 on v0

--- a/solution.py
+++ b/solution.py
@@ -1,12 +1,17 @@
+import functools
 import math
 
 import jax
 import jax.numpy as jnp
 from jax import lax
+from jax.experimental import pallas as pl
+from jax.experimental.pallas import tpu as pltpu
 from jax.sharding import PartitionSpec as P
 
 INNER = 3
 OUTER = 2
+MESH = pl.DeviceIdType.MESH
+HIGH = lax.Precision.HIGHEST
 
 
 def kernel_tile(col_feat, col_norm, row_feat, row_norm):
@@ -33,7 +38,7 @@
     return lax.fori_loop(0, columns // sub_cols, advance, running)
 
 
-def body(features, targets, point_order, lengthscale, noise_var):
+def body_large(features, targets, point_order, lengthscale, noise_var):
     scaled = features / lengthscale[:, None]
     row_norms = jnp.sum(scaled * scaled, 0)
     block_feat, block_targ = (
@@ -95,9 +100,266 @@
     return (solution, residual)
 
 
+def to_column(row, rhs):
+    shape = (rhs, row.shape[1])
+    on_diag = lax.broadcasted_iota(jnp.int32, shape, 0) == lax.broadcasted_iota(jnp.int32, shape, 1)
+    return jnp.sum(jnp.where(on_diag, row, 0.0), 1, keepdims=True)
+
+
+def to_row(column, lanes):
+    shape = (column.shape[0], lanes)
+    on_diag = lax.broadcasted_iota(jnp.int32, shape, 0) == lax.broadcasted_iota(jnp.int32, shape, 1)
+    return jnp.sum(jnp.where(on_diag, column, 0.0), 0, keepdims=True)
+
+
+def fused(
+    n_rows,
+    n_cols,
+    feat_ref,
+    targ_ref,
+    order_ref,
+    length_ref,
+    noise_ref,
+    sol_ref,
+    res_ref,
+    parts,
+    feats,
+    tiles,
+    corrs,
+    sums,
+    part_send,
+    part_recv,
+    feat_send,
+    feat_recv,
+    corr_send,
+    corr_recv,
+    sum_send,
+    sum_recv,
+):
+    row, col = lax.axis_index("rows"), lax.axis_index("cols")
+    n_feats, own_len = feat_ref.shape
+    rhs = targ_ref.shape[0]
+    block = n_cols * own_len
+
+    def row_peer(k):
+        return lax.rem(row + k, n_rows)
+
+    def col_peer(k):
+        return lax.rem(col + k, n_cols)
+
+    def each(count, step):
+        def one(k, carry):
+            step(k)
+            return carry
+
+        lax.fori_loop(1, count, one, 0)
+
+    barrier = pltpu.get_barrier_semaphore()
+    each(
+        n_cols,
+        lambda k: pl.semaphore_signal(
+            barrier, inc=1, device_id=(row, col_peer(k)), device_id_type=MESH
+        ),
+    )
+    each(
+        n_rows,
+        lambda k: pl.semaphore_signal(
+            barrier, inc=1, device_id=(row_peer(k), col), device_id_type=MESH
+        ),
+    )
+
+    noise_col = to_column(noise_ref[...], rhs)
+    scaled = feat_ref[...] / to_column(length_ref[...], n_feats)
+    order = (order_ref[...] - row * block).astype(jnp.float32)
+    own = jnp.concatenate(
+        [scaled, targ_ref[...], jnp.broadcast_to(order, (8, own_len))], axis=0
+    )
+    wide = jnp.concatenate([own] * n_cols, axis=1)
+    lane = lax.broadcasted_iota(jnp.int32, wide.shape, 1)
+    parts[col] = jnp.where(lane // own_len == col, wide, 0.0)
+    pl.semaphore_wait(barrier, n_rows - 1 + n_cols - 1)
+
+    def part_copy(k, slot):
+        return pltpu.make_async_remote_copy(
+            src_ref=parts.at[slot],
+            dst_ref=parts.at[slot],
+            send_sem=part_send.at[k],
+            recv_sem=part_recv.at[k],
+            device_id=(row, col_peer(k)),
+            device_id_type=MESH,
+        )
+
+    each(n_cols, lambda k: part_copy(k, col).start())
+    each(n_cols, lambda k: part_copy(k, col_peer(n_cols - k)).wait_recv())
+    whole = parts[0]
+    for c in range(1, n_cols):
+        whole = whole + parts[c]
+    block_feat = whole[:n_feats]
+    block_targ = whole[n_feats : n_feats + rhs]
+    block_order = whole[n_feats + rhs : n_feats + rhs + 1]
+    feats[row] = block_feat
+
+    def feat_copy(k, slot):
+        return pltpu.make_async_remote_copy(
+            src_ref=feats.at[slot],
+            dst_ref=feats.at[slot],
+            send_sem=feat_send.at[k],
+            recv_sem=feat_recv.at[k],
+            device_id=(row_peer(k), col),
+            device_id_type=MESH,
+        )
+
+    each(n_rows, lambda k: feat_copy(k, row).start())
+
+    place = lax.broadcasted_iota(jnp.int32, (block, block), 0).astype(jnp.float32)
+    picked = jnp.where(place == block_order, 1.0, 0.0)
+    residual = jnp.dot(block_targ, picked, precision=HIGH, preferred_element_type=jnp.float32)
+
+    own_feat = jnp.transpose(block_feat)
+    own_norm = jnp.sum(own_feat * own_feat, 1, keepdims=True)
+
+    def tile_of(feat):
+        norm = jnp.sum(feat * feat, 0, keepdims=True)
+        inner_prod = jnp.dot(own_feat, feat, precision=HIGH, preferred_element_type=jnp.float32)
+        return jnp.exp(-0.5 * (own_norm + norm - 2.0 * inner_prod)).astype(jnp.bfloat16)
+
+    block_tile = tile_of(block_feat)
+
+    def solve(residual):
+        remains = residual
+        res_norm = jnp.sum(remains * remains, 1, keepdims=True)
+        direction = remains
+        correction = jnp.zeros_like(remains)
+        for inner_turn in range(INNER):
+            image = (
+                jnp.dot(
+                    direction.astype(jnp.bfloat16), block_tile, preferred_element_type=jnp.float32
+                )
+                + noise_col * direction
+            )
+            step_len = res_norm / jnp.sum(direction * image, 1, keepdims=True)
+            correction = correction + step_len * direction
+            if inner_turn + 1 < INNER:
+                remains = remains - step_len * image
+                new_norm = jnp.sum(remains * remains, 1, keepdims=True)
+                direction = remains + (new_norm / res_norm) * direction
+                res_norm = new_norm
+        return correction
+
+    def corr_copy(turn, k, slot):
+        return pltpu.make_async_remote_copy(
+            src_ref=corrs.at[turn, slot],
+            dst_ref=corrs.at[turn, slot],
+            send_sem=corr_send.at[turn, k],
+            recv_sem=corr_recv.at[turn, k],
+            device_id=(row_peer(k), col),
+            device_id_type=MESH,
+        )
+
+    def sum_copy(turn, k, slot):
+        return pltpu.make_async_remote_copy(
+            src_ref=sums.at[turn, slot],
+            dst_ref=sums.at[turn, slot],
+            send_sem=sum_send.at[turn, k],
+            recv_sem=sum_recv.at[turn, k],
+            device_id=(row_peer(k), col),
+            device_id_type=MESH,
+        )
+
+    solved = jnp.zeros_like(residual)
+    for turn in range(OUTER):
+        correction = solve(residual)
+        corrs[turn, row] = correction.astype(jnp.bfloat16)
+        each(n_rows, lambda k: corr_copy(turn, k, row).start())
+        if turn == 0:
+            each(n_rows, lambda k: feat_copy(k, row_peer(n_rows - k)).wait_recv())
+            for b in range(n_rows):
+                tiles[b] = tile_of(feats[b])
+        each(n_rows, lambda k: corr_copy(turn, k, row_peer(n_rows - k)).wait_recv())
+        applied = noise_col * correction
+        for b in range(n_rows):
+            applied = applied + lax.dot_general(
+                corrs[turn, b],
+                tiles[b],
+                (((1,), (1,)), ((), ())),
+                preferred_element_type=jnp.float32,
+            )
+        lanes = sums.shape[-1]
+        cross = to_row(jnp.sum(residual * applied, 1, keepdims=True), lanes)
+        energy = to_row(jnp.sum(applied * applied, 1, keepdims=True), lanes)
+        sums[turn, row] = jnp.concatenate([cross, energy], axis=0)
+        each(n_rows, lambda k: sum_copy(turn, k, row).start())
+        each(n_rows, lambda k: sum_copy(turn, k, row_peer(n_rows - k)).wait_recv())
+        total = jnp.sum(sums[turn], 0)
+        damping = to_column(total[0:1] / (total[1:2] + 1e-06), rhs)
+        solved = solved + damping * correction
+        residual = residual - damping * applied
+
+    def own_part(field):
+        picked_part = field[:, :own_len]
+        for c in range(1, n_cols):
+            picked_part = jnp.where(
+                col == c, field[:, c * own_len : (c + 1) * own_len], picked_part
+            )
+        return picked_part
+
+    sol_ref[...] = own_part(solved)
+    res_ref[...] = own_part(residual)
+    each(n_cols, lambda k: part_copy(k, col).wait_send())
+    each(n_rows, lambda k: feat_copy(k, row).wait_send())
+    for turn in range(OUTER):
+        each(n_rows, lambda k: corr_copy(turn, k, row).wait_send())
+        each(n_rows, lambda k: sum_copy(turn, k, row).wait_send())
+
+
+def body_small(n_rows, n_cols, features, targets, point_order, lengthscale, noise_var):
+    n_feats, own_len = features.shape
+    rhs = targets.shape[0]
+    block = n_cols * own_len
+    out = jax.ShapeDtypeStruct((rhs, own_len), jnp.float32)
+    vmem = pl.BlockSpec(memory_space=pltpu.VMEM)
+    dma = pltpu.SemaphoreType.DMA
+    return pl.pallas_call(
+        functools.partial(fused, n_rows, n_cols),
+        out_shape=(out, out),
+        in_specs=[vmem] * 5,
+        out_specs=(vmem, vmem),
+        scratch_shapes=[
+            pltpu.VMEM((n_cols, n_feats + rhs + 8, block), jnp.float32),
+            pltpu.VMEM((n_rows, n_feats, block), jnp.float32),
+            pltpu.VMEM((n_rows, block, block), jnp.bfloat16),
+            pltpu.VMEM((OUTER, n_rows, rhs, block), jnp.bfloat16),
+            pltpu.VMEM((OUTER, n_rows, 2, 128), jnp.float32),
+            dma((n_cols,)),
+            dma((n_cols,)),
+            dma((n_rows,)),
+            dma((n_rows,)),
+            dma((OUTER, n_rows)),
+            dma((OUTER, n_rows)),
+            dma((OUTER, n_rows)),
+            dma((OUTER, n_rows)),
+        ],
+        compiler_params=pltpu.CompilerParams(
+            collective_id=0, has_side_effects=True, vmem_limit_bytes=32 * 1024 * 1024
+        ),
+    )(features, targets, point_order[None, :], lengthscale[None, :], noise_var[None, :])
+
+
+def body(n_rows, n_cols, features, targets, point_order, lengthscale, noise_var):
+    n_feats, own_len = features.shape
+    rhs = targets.shape[0]
+    block = n_cols * own_len
+    args = (features, targets, point_order, lengthscale, noise_var)
+    fits = 2 * n_rows * block * block <= 8 * 1024 * 1024
+    even = block % 128 == 0 and rhs % 16 == 0 and rhs <= 128 and n_feats % 8 == 0
+    if fits and even and n_rows > 1 and n_cols > 1:
+        return body_small(n_rows, n_cols, *args)
+    return body_large(*args)
+
+
 def solution(mesh):
     return jax.shard_map(
-        body,
+        functools.partial(body, mesh.shape["rows"], mesh.shape["cols"]),
         mesh=mesh,
         in_specs=(
             P(None, ("rows", "cols")),

time: 219 us -> 39.1 us (0.18)
  blocking collectives: 204 us -> 0 us
  Pallas kernels: 0 us -> 34.8 us
  matrix products: 5.49 us -> 0 us
  other arithmetic: 3.3 us -> 0 us
    all_gather x7 -> x0, blocking collectives: 131 us -> none  [the longest x2 85.9 us: body(): lax.all_gather(packed, ('rows', 'cols'), axis=1, tiled=True)]
    psum x2 -> x0, blocking collectives: 73.9 us -> none  [body(): lax.psum((jnp.sum(residual * applied, 1), jnp.sum(applied * applied, 1)),...]
    pallas_call x0 -> x1, Pallas kernels: none -> 34.8 us  [body_small(): pl.pallas_call(functools.partial(fused, n_rows, n_cols), out_shape=(out,...]
    dot_general x23 -> x0, matrix products: 5.49 us -> none  [the longest x9 2.96 us: kernel_tile(): jnp.dot(col_feat.T, row_feat, precision=lax.Precision.HIGHEST, preferred_...]
where the time goes in v1:
time: 39.1 us; the launch traced here: 38.7 us
  Pallas kernels  34.8 us (89%)
  local copies, waits for them, and re-layouts  3.29 us (8%)
  between operations  0.67 us (2%)
    pallas_call x1, Pallas kernels, body_small(): pl.pallas_call(functools.partial(fused, n_rows, n_cols), out_shape=(out,...  34.8 us
    unnamed x12, local copies, waits for them, and re-layouts  3.29 us

profile of v1, /device:TPU:0, one launch (start us, length us, event | category | flops | bytes accessed | tf_op | source)
XLA Modules:
  0.0 38.7 jit_solution(13665694164402153844)
XLA Ops:
  0.6 0.0 copy-start.2
  0.6 0.0 copy-start.3
  0.7 0.0 copy-start.4
  0.7 0.6 %copy-done.2 = s32[64]{0:T(128)S(1)} copy-done((s32[64]{0:T(128)S(1)}, s32[64]{0:T(128)}, u32[]{:S(2)}) %copy-start.2) | copy-done | bytes 280
  1.3 0.0 copy-done.3
  1.3 0.0 copy-done.4
  1.3 0.0 copy-start
  1.3 0.7 %copy-done = f32[32,64]{1,0:T(8,128)S(1)} copy-done((f32[32,64]{1,0:T(8,128)S(1)}, f32[32,64]{1,0:T(8,128)}, u32[]{:S(2)}) %copy-start) | copy-done | bytes 8216
  2.0 0.0 copy-start.1
  2.0 0.7 %copy-done.1 = f32[16,64]{1,0:T(8,128)S(1)} copy-done((f32[16,64]{1,0:T(8,128)S(1)}, f32[16,64]{1,0:T(8,128)}, u32[]{:S(2)}) %copy-start.1) | copy-done | bytes 4120
  2.7 34.8 %shard_map.68 = (f32[32,64]{1,0:T(8,128)S(1)}, f32[32,64]{1,0:T(8,128)S(1)}) custom-call(f32[16,64]{1,0:T(8,128)S(1)} %copy-done.1, f32[32,64]{1,0:T(8,128)S(1)} %copy-done, s32[1,64]{1,0:T(1,128)S(1)} %bitcast.3, f32[1,16]{1,0:T(1,128)S(1)} %bitcast.4, f32[1,32]{1,0:T(1,128)S(1)} %bitcast.5), custom_call_target="tpu_custom_call" | custom-call | tf_op jit(solution)/shard_map/pallas_call | solution.py:322
  37.5 0.6 %copy.9 = f32[32,64]{1,0:T(8,128)} copy(f32[32,64]{1,0:T(8,128)S(1)} %get-tuple-element.4) | data formatting | bytes 16384
  38.1 0.6 %copy.10 = f32[32,64]{1,0:T(8,128)} copy(f32[32,64]{1,0:T(8,128)S(1)} %get-tuple-element.5) | data formatting | bytes 16384
Async XLA Ops:
  0.6 0.7 %copy-start.2 = (s32[64]{0:T(128)S(1)}, s32[64]{0:T(128)}, u32[]{:S(2)}) copy-start(s32[64]{0:T(128)} %param.7) | copy-start | bytes 772
  0.6 0.7 %copy-start.3 = (f32[16]{0:T(128)S(1)}, f32[16]{0:T(128)}, u32[]{:S(2)}) copy-start(f32[16]{0:T(128)} %param.8) | copy-start | bytes 196
  0.7 0.7 %copy-start.4 = (f32[32]{0:T(128)S(1)}, f32[32]{0:T(128)}, u32[]{:S(2)}) copy-start(f32[32]{0:T(128)} %param.9) | copy-start | bytes 388
  1.3 0.7 %copy-start = (f32[32,64]{1,0:T(8,128)S(1)}, f32[32,64]{1,0:T(8,128)}, u32[]{:S(2)}) copy-start(f32[32,64]{1,0:T(8,128)} %targ_ref.1) | copy-start | bytes 24580
  2.0 0.7 %copy-start.1 = (f32[16,64]{1,0:T(8,128)S(1)}, f32[16,64]{1,0:T(8,128)}, u32[]{:S(2)}) copy-start(f32[16,64]{1,0:T(8,128)} %feat_ref.1) | copy-start | bytes 12292

commit v2 on v1

--- a/solution.py
+++ b/solution.py
@@ -11,7 +11,6 @@
 INNER = 3
 OUTER = 2
 MESH = pl.DeviceIdType.MESH
-HIGH = lax.Precision.HIGHEST
 
 
 def kernel_tile(col_feat, col_norm, row_feat, row_norm):
@@ -100,33 +99,51 @@
     return (solution, residual)
 
 
-def to_column(row, rhs):
-    shape = (rhs, row.shape[1])
-    on_diag = lax.broadcasted_iota(jnp.int32, shape, 0) == lax.broadcasted_iota(jnp.int32, shape, 1)
-    return jnp.sum(jnp.where(on_diag, row, 0.0), 1, keepdims=True)
-
-
-def to_row(column, lanes):
-    shape = (column.shape[0], lanes)
-    on_diag = lax.broadcasted_iota(jnp.int32, shape, 0) == lax.broadcasted_iota(jnp.int32, shape, 1)
-    return jnp.sum(jnp.where(on_diag, column, 0.0), 0, keepdims=True)
+def to_column(row, rows, first=0):
+    shape = (rows, row.shape[1])
+    at, lane = (lax.broadcasted_iota(jnp.int32, shape, axis) for axis in (0, 1))
+    return jnp.sum(jnp.where(at + first == lane, row, 0.0), 1, keepdims=True)
+
+
+def to_row(columns, lanes):
+    rows = columns[0].shape[0]
+    at, lane = (lax.broadcasted_iota(jnp.int32, (rows, lanes), axis) for axis in (0, 1))
+    placed = jnp.zeros((rows, lanes), jnp.float32)
+    for which, column in enumerate(columns):
+        placed = jnp.where(at + which * rows == lane, column, placed)
+    return jnp.sum(placed, 0, keepdims=True)
+
+
+def three_parts(x):
+    high = x.astype(jnp.bfloat16).astype(jnp.float32)
+    mid = (x - high).astype(jnp.bfloat16).astype(jnp.float32)
+    low = ((x - high) - mid).astype(jnp.bfloat16).astype(jnp.float32)
+    return high, mid, low
 
 
 def fused(
     n_rows,
     n_cols,
+    feat_hbm,
+    targ_hbm,
+    order_hbm,
+    length_hbm,
+    noise_hbm,
+    sol_ref,
+    res_ref,
     feat_ref,
     targ_ref,
     order_ref,
     length_ref,
     noise_ref,
-    sol_ref,
-    res_ref,
+    parts_out,
     parts,
     feats,
     tiles,
     corrs,
     sums,
+    ends,
+    load_sem,
     part_send,
     part_recv,
     feat_send,
@@ -135,10 +152,12 @@
     corr_recv,
     sum_send,
     sum_recv,
+    end_send,
+    end_recv,
 ):
     row, col = lax.axis_index("rows"), lax.axis_index("cols")
     n_feats, own_len = feat_ref.shape
-    rhs = targ_ref.shape[0]
+    own_rhs = targ_ref.shape[0] // n_cols
     block = n_cols * own_len
 
     def row_peer(k):
@@ -153,6 +172,21 @@
             return carry
 
         lax.fori_loop(1, count, one, 0)
+
+    loads = [
+        pltpu.make_async_copy(source, target, load_sem.at[which])
+        for which, (source, target) in enumerate(
+            (
+                (feat_hbm, feat_ref),
+                (targ_hbm, targ_ref),
+                (order_hbm, order_ref),
+                (length_hbm, length_ref),
+                (noise_hbm, noise_ref),
+            )
+        )
+    ]
+    for load in loads:
+        load.start()
 
     barrier = pltpu.get_barrier_semaphore()
     each(
@@ -167,60 +201,82 @@
             barrier, inc=1, device_id=(row_peer(k), col), device_id_type=MESH
         ),
     )
-
-    noise_col = to_column(noise_ref[...], rhs)
+    for load in loads:
+        load.wait()
+
+    noise_col = to_column(noise_ref[...], own_rhs, col * own_rhs)
     scaled = feat_ref[...] / to_column(length_ref[...], n_feats)
     order = (order_ref[...] - row * block).astype(jnp.float32)
-    own = jnp.concatenate(
-        [scaled, targ_ref[...], jnp.broadcast_to(order, (8, own_len))], axis=0
-    )
-    wide = jnp.concatenate([own] * n_cols, axis=1)
-    lane = lax.broadcasted_iota(jnp.int32, wide.shape, 1)
-    parts[col] = jnp.where(lane // own_len == col, wide, 0.0)
+    order = jnp.broadcast_to(order, (8, own_len))
+    for c in range(n_cols):
+        share = targ_ref[c * own_rhs : (c + 1) * own_rhs, :]
+        own = jnp.concatenate([scaled, share, order], axis=0)
+        wide = jnp.concatenate([own] * n_cols, axis=1)
+        lane = lax.broadcasted_iota(jnp.int32, wide.shape, 1)
+        parts_out[c] = jnp.where(lane // own_len == col, wide, 0.0)
     pl.semaphore_wait(barrier, n_rows - 1 + n_cols - 1)
 
-    def part_copy(k, slot):
+    def part_copy(k, target, slot):
         return pltpu.make_async_remote_copy(
-            src_ref=parts.at[slot],
+            src_ref=parts_out.at[target],
             dst_ref=parts.at[slot],
             send_sem=part_send.at[k],
             recv_sem=part_recv.at[k],
-            device_id=(row, col_peer(k)),
+            device_id=(row, target),
             device_id_type=MESH,
         )
 
-    each(n_cols, lambda k: part_copy(k, col).start())
-    each(n_cols, lambda k: part_copy(k, col_peer(n_cols - k)).wait_recv())
+    each(n_cols, lambda k: part_copy(k, col_peer(k), col).start())
+    parts[col] = parts_out[col]
+    each(n_cols, lambda k: part_copy(k, col_peer(k), col_peer(n_cols - k)).wait_recv())
     whole = parts[0]
     for c in range(1, n_cols):
         whole = whole + parts[c]
     block_feat = whole[:n_feats]
-    block_targ = whole[n_feats : n_feats + rhs]
-    block_order = whole[n_feats + rhs : n_feats + rhs + 1]
+    block_targ = whole[n_feats : n_feats + own_rhs]
+    block_order = whole[n_feats + own_rhs : n_feats + own_rhs + 1]
     feats[row] = block_feat
 
-    def feat_copy(k, slot):
+    def row_copy(buffer, send_sem, recv_sem, k, slot):
         return pltpu.make_async_remote_copy(
-            src_ref=feats.at[slot],
-            dst_ref=feats.at[slot],
-            send_sem=feat_send.at[k],
-            recv_sem=feat_recv.at[k],
+            src_ref=buffer.at[slot],
+            dst_ref=buffer.at[slot],
+            send_sem=send_sem.at[k],
+            recv_sem=recv_sem.at[k],
             device_id=(row_peer(k), col),
             device_id_type=MESH,
         )
 
-    each(n_rows, lambda k: feat_copy(k, row).start())
+    def spread(*copy):
+        each(n_rows, lambda k: row_copy(*copy, k, row).start())
+
+    def arrive(*copy):
+        each(n_rows, lambda k: row_copy(*copy, k, row_peer(n_rows - k)).wait_recv())
+
+    feat_args = (feats, feat_send, feat_recv)
+    corr_args = [(corrs.at[t], corr_send.at[t], corr_recv.at[t]) for t in range(OUTER)]
+    sum_args = [(sums.at[t], sum_send.at[t], sum_recv.at[t]) for t in range(OUTER)]
+
+    spread(*feat_args)
 
     place = lax.broadcasted_iota(jnp.int32, (block, block), 0).astype(jnp.float32)
-    picked = jnp.where(place == block_order, 1.0, 0.0)
-    residual = jnp.dot(block_targ, picked, precision=HIGH, preferred_element_type=jnp.float32)
-
-    own_feat = jnp.transpose(block_feat)
-    own_norm = jnp.sum(own_feat * own_feat, 1, keepdims=True)
+    picked = jnp.where(place == block_order, 1.0, 0.0).astype(jnp.bfloat16)
+    three = jnp.concatenate(three_parts(block_targ), axis=0).astype(jnp.bfloat16)
+    three = jnp.dot(three, picked, preferred_element_type=jnp.float32)
+    residual = (three[:own_rhs] + three[own_rhs : 2 * own_rhs]) + three[2 * own_rhs :]
+
+    high, mid, low = three_parts(block_feat)
+    own_stack = jnp.transpose(jnp.concatenate([high, high, mid, mid, high, low], axis=0))
+    own_stack = own_stack.astype(jnp.bfloat16)
+    own_norm = jnp.transpose(
+        jnp.broadcast_to(jnp.sum(block_feat * block_feat, 0, keepdims=True), (8, block))
+    )[:, :1]
 
     def tile_of(feat):
         norm = jnp.sum(feat * feat, 0, keepdims=True)
-        inner_prod = jnp.dot(own_feat, feat, precision=HIGH, preferred_element_type=jnp.float32)
+        high, mid, low = three_parts(feat)
+        stack = jnp.concatenate([high, mid, high, mid, low, high], axis=0).astype(jnp.bfloat16)
+        inner_prod = jnp.dot(own_stack, stack, preferred_element_type=jnp.float32)
         return jnp.exp(-0.5 * (own_norm + norm - 2.0 * inner_prod)).astype(jnp.bfloat16)
 
     block_tile = tile_of(block_feat)
@@ -246,90 +302,84 @@
                 res_norm = new_norm
         return correction
 
-    def corr_copy(turn, k, slot):
-        return pltpu.make_async_remote_copy(
-            src_ref=corrs.at[turn, slot],
-            dst_ref=corrs.at[turn, slot],
-            send_sem=corr_send.at[turn, k],
-            recv_sem=corr_recv.at[turn, k],
-            device_id=(row_peer(k), col),
-            device_id_type=MESH,
-        )
-
-    def sum_copy(turn, k, slot):
-        return pltpu.make_async_remote_copy(
-            src_ref=sums.at[turn, slot],
-            dst_ref=sums.at[turn, slot],
-            send_sem=sum_send.at[turn, k],
-            recv_sem=sum_recv.at[turn, k],
-            device_id=(row_peer(k), col),
-            device_id_type=MESH,
-        )
-
     solved = jnp.zeros_like(residual)
     for turn in range(OUTER):
         correction = solve(residual)
         corrs[turn, row] = correction.astype(jnp.bfloat16)
-        each(n_rows, lambda k: corr_copy(turn, k, row).start())
+        spread(*corr_args[turn])
         if turn == 0:
-            each(n_rows, lambda k: feat_copy(k, row_peer(n_rows - k)).wait_recv())
+            arrive(*feat_args)
             for b in range(n_rows):
-                tiles[b] = tile_of(feats[b])
-        each(n_rows, lambda k: corr_copy(turn, k, row_peer(n_rows - k)).wait_recv())
-        applied = noise_col * correction
-        for b in range(n_rows):
-            applied = applied + lax.dot_general(
-                corrs[turn, b],
-                tiles[b],
-                (((1,), (1,)), ((), ())),
-                preferred_element_type=jnp.float32,
-            )
-        lanes = sums.shape[-1]
-        cross = to_row(jnp.sum(residual * applied, 1, keepdims=True), lanes)
-        energy = to_row(jnp.sum(applied * applied, 1, keepdims=True), lanes)
-        sums[turn, row] = jnp.concatenate([cross, energy], axis=0)
-        each(n_rows, lambda k: sum_copy(turn, k, row).start())
-        each(n_rows, lambda k: sum_copy(turn, k, row_peer(n_rows - k)).wait_recv())
+                tiles[:, b * block : (b + 1) * block] = tile_of(feats[b])
+        arrive(*corr_args[turn])
+        everyone = jnp.concatenate([corrs[turn, b] for b in range(n_rows)], axis=1)
+        applied = noise_col * correction + lax.dot_general(
+            everyone, tiles[...], (((1,), (1,)), ((), ())), preferred_element_type=jnp.float32
+        )
+        cross = jnp.sum(residual * applied, 1, keepdims=True)
+        energy = jnp.sum(applied * applied, 1, keepdims=True)
+        sums[turn, row] = to_row((cross, energy), sums.shape[-1])
+        spread(*sum_args[turn])
+        arrive(*sum_args[turn])
         total = jnp.sum(sums[turn], 0)
-        damping = to_column(total[0:1] / (total[1:2] + 1e-06), rhs)
+        damping = to_column(total, own_rhs) / (to_column(total, own_rhs, own_rhs) + 1e-06)
         solved = solved + damping * correction
         residual = residual - damping * applied
 
-    def own_part(field):
-        picked_part = field[:, :own_len]
+    def end_copy(k, slot):
+        return pltpu.make_async_remote_copy(
+            src_ref=ends.at[slot],
+            dst_ref=ends.at[slot],
+            send_sem=end_send.at[k],
+            recv_sem=end_recv.at[k],
+            device_id=(row, col_peer(k)),
+            device_id_type=MESH,
+        )
+
+    ends[col, 0] = solved
+    ends[col, 1] = residual
+    each(n_cols, lambda k: end_copy(k, col).start())
+
+    each(n_cols, lambda k: part_copy(k, col_peer(k), col).wait_send())
+    for copy in (feat_args, *corr_args, *sum_args):
+        each(n_rows, lambda k: row_copy(*copy, k, row).wait_send())
+
+    def own_points(field):
+        points = field[:, :own_len]
         for c in range(1, n_cols):
-            picked_part = jnp.where(
-                col == c, field[:, c * own_len : (c + 1) * own_len], picked_part
-            )
-        return picked_part
-
-    sol_ref[...] = own_part(solved)
-    res_ref[...] = own_part(residual)
-    each(n_cols, lambda k: part_copy(k, col).wait_send())
-    each(n_rows, lambda k: feat_copy(k, row).wait_send())
-    for turn in range(OUTER):
-        each(n_rows, lambda k: corr_copy(turn, k, row).wait_send())
-        each(n_rows, lambda k: sum_copy(turn, k, row).wait_send())
+            points = jnp.where(col == c, field[:, c * own_len : (c + 1) * own_len], points)
+        return points
+
+    each(n_cols, lambda k: end_copy(k, col_peer(n_cols - k)).wait_recv())
+    for c in range(n_cols):
+        sol_ref[c * own_rhs : (c + 1) * own_rhs, :] = own_points(ends[c, 0])
+        res_ref[c * own_rhs : (c + 1) * own_rhs, :] = own_points(ends[c, 1])
+    each(n_cols, lambda k: end_copy(k, col).wait_send())
 
 
 def body_small(n_rows, n_cols, features, targets, point_order, lengthscale, noise_var):
     n_feats, own_len = features.shape
     rhs = targets.shape[0]
+    own_rhs = rhs // n_cols
     block = n_cols * own_len
     out = jax.ShapeDtypeStruct((rhs, own_len), jnp.float32)
-    vmem = pl.BlockSpec(memory_space=pltpu.VMEM)
+    args = (features, targets, point_order[None, :], lengthscale[None, :], noise_var[None, :])
     dma = pltpu.SemaphoreType.DMA
     return pl.pallas_call(
         functools.partial(fused, n_rows, n_cols),
         out_shape=(out, out),
-        in_specs=[vmem] * 5,
-        out_specs=(vmem, vmem),
+        in_specs=[pl.BlockSpec(memory_space=pl.ANY)] * len(args),
+        out_specs=(pl.BlockSpec(memory_space=pltpu.VMEM),) * 2,
         scratch_shapes=[
-            pltpu.VMEM((n_cols, n_feats + rhs + 8, block), jnp.float32),
+            *(pltpu.VMEM(arg.shape, arg.dtype) for arg in args),
+            pltpu.VMEM((n_cols, n_feats + own_rhs + 8, block), jnp.float32),
+            pltpu.VMEM((n_cols, n_feats + own_rhs + 8, block), jnp.float32),
             pltpu.VMEM((n_rows, n_feats, block), jnp.float32),
-            pltpu.VMEM((n_rows, block, block), jnp.bfloat16),
-            pltpu.VMEM((OUTER, n_rows, rhs, block), jnp.bfloat16),
-            pltpu.VMEM((OUTER, n_rows, 2, 128), jnp.float32),
+            pltpu.VMEM((block, n_rows * block), jnp.bfloat16),
+            pltpu.VMEM((OUTER, n_rows, own_rhs, block), jnp.bfloat16),
+            pltpu.VMEM((OUTER, n_rows, 1, 128), jnp.float32),
+            pltpu.VMEM((n_cols, 2, own_rhs, block), jnp.float32),
+            dma((len(args),)),
             dma((n_cols,)),
             dma((n_cols,)),
             dma((n_rows,)),
@@ -338,11 +388,13 @@
             dma((OUTER, n_rows)),
             dma((OUTER, n_rows)),
             dma((OUTER, n_rows)),
+            dma((n_cols,)),
+            dma((n_cols,)),
         ],
         compiler_params=pltpu.CompilerParams(
             collective_id=0, has_side_effects=True, vmem_limit_bytes=32 * 1024 * 1024
         ),
-    )(features, targets, point_order[None, :], lengthscale[None, :], noise_var[None, :])
+    )(*args)
 
 
 def body(n_rows, n_cols, features, targets, point_order, lengthscale, noise_var):
@@ -351,7 +403,8 @@
     block = n_cols * own_len
     args = (features, targets, point_order, lengthscale, noise_var)
     fits = 2 * n_rows * block * block <= 8 * 1024 * 1024
-    even = block % 128 == 0 and rhs % 16 == 0 and rhs <= 128 and n_feats % 8 == 0
+    even = block % 128 == 0 and rhs % (16 * n_cols) == 0 and n_feats % 8 == 0
+    even = even and 2 * rhs // n_cols <= 128
     if fits and even and n_rows > 1 and n_cols > 1:
         return body_small(n_rows, n_cols, *args)
     return body_large(*args)

time: 39.1 us -> 36.4 us (0.931)
  Pallas kernels: 34.8 us -> 32.1 us
    pallas_call x1, Pallas kernels: 34.8 us -> 32.1 us  [body_small(): pl.pallas_call(functools.partial(fused, n_rows, n_cols), out_shape=(out,...]
where the time goes in v2:
time: 36.4 us; the launch traced here: 36 us
  Pallas kernels  32.1 us (88%)
  local copies, waits for them, and re-layouts  3.29 us (9%)
  between operations  0.67 us (2%)
    pallas_call x1, Pallas kernels, body_small(): pl.pallas_call(functools.partial(fused, n_rows, n_cols), out_shape=(out,...  32.1 us
    unnamed x12, local copies, waits for them, and re-layouts  3.29 us

profile of v2, /device:TPU:0, one launch (start us, length us, event | category | flops | bytes accessed | tf_op | source)
XLA Modules:
  0.0 36.0 jit_solution(11259975214989533658)
XLA Ops:
  0.6 0.0 copy-start.2
  0.6 0.0 copy-start.3
  0.7 0.0 copy-start.4
  0.7 0.6 %copy-done.2 = s32[64]{0:T(128)S(1)} copy-done((s32[64]{0:T(128)S(1)}, s32[64]{0:T(128)}, u32[]{:S(2)}) %copy-start.2) | copy-done | bytes 280
  1.3 0.0 copy-done.3
  1.3 0.0 copy-done.4
  1.3 0.0 copy-start
  1.3 0.7 %copy-done = f32[32,64]{1,0:T(8,128)S(1)} copy-done((f32[32,64]{1,0:T(8,128)S(1)}, f32[32,64]{1,0:T(8,128)}, u32[]{:S(2)}) %copy-start) | copy-done | bytes 8216
  2.0 0.0 copy-start.1
  2.0 0.7 %copy-done.1 = f32[16,64]{1,0:T(8,128)S(1)} copy-done((f32[16,64]{1,0:T(8,128)S(1)}, f32[16,64]{1,0:T(8,128)}, u32[]{:S(2)}) %copy-start.1) | copy-done | bytes 4120
  2.7 32.1 %shard_map.68 = (f32[32,64]{1,0:T(8,128)S(1)}, f32[32,64]{1,0:T(8,128)S(1)}) custom-call(f32[16,64]{1,0:T(8,128)S(1)} %copy-done.1, f32[32,64]{1,0:T(8,128)S(1)} %copy-done, s32[1,64]{1,0:T(1,128)S(1)} %bitcast.3, f32[1,16]{1,0:T(1,128)S(1)} %bitcast.4, f32[1,32]{1,0:T(1,128)S(1)} %bitcast.5), custom_call_target="tpu_custom_call" | custom-call | tf_op jit(solution)/shard_map/pallas_call | solution.py:368
  34.8 0.6 %copy.9 = f32[32,64]{1,0:T(8,128)} copy(f32[32,64]{1,0:T(8,128)S(1)} %get-tuple-element.4) | data formatting | bytes 16384
  35.4 0.6 %copy.10 = f32[32,64]{1,0:T(8,128)} copy(f32[32,64]{1,0:T(8,128)S(1)} %get-tuple-element.5) | data formatting | bytes 16384
Async XLA Ops:
  0.6 0.7 %copy-start.2 = (s32[64]{0:T(128)S(1)}, s32[64]{0:T(128)}, u32[]{:S(2)}) copy-start(s32[64]{0:T(128)} %param.7) | copy-start | bytes 772
  0.6 0.7 %copy-start.3 = (f32[16]{0:T(128)S(1)}, f32[16]{0:T(128)}, u32[]{:S(2)}) copy-start(f32[16]{0:T(128)} %param.8) | copy-start | bytes 196
  0.7 0.7 %copy-start.4 = (f32[32]{0:T(128)S(1)}, f32[32]{0:T(128)}, u32[]{:S(2)}) copy-start(f32[32]{0:T(128)} %param.9) | copy-start | bytes 388
  1.3 0.7 %copy-start = (f32[32,64]{1,0:T(8,128)S(1)}, f32[32,64]{1,0:T(8,128)}, u32[]{:S(2)}) copy-start(f32[32,64]{1,0:T(8,128)} %targ_hbm.1) | copy-start | bytes 24580
  2.0 0.7 %copy-start.1 = (f32[16,64]{1,0:T(8,128)S(1)}, f32[16,64]{1,0:T(8,128)}, u32[]{:S(2)}) copy-start(f32[16,64]{1,0:T(8,128)} %feat_hbm.1) | copy-start | bytes 12292

commit v3 on v2

--- a/solution.py
+++ b/solution.py
@@ -105,15 +105,6 @@
     return jnp.sum(jnp.where(at + first == lane, row, 0.0), 1, keepdims=True)
 
 
-def to_row(columns, lanes):
-    rows = columns[0].shape[0]
-    at, lane = (lax.broadcasted_iota(jnp.int32, (rows, lanes), axis) for axis in (0, 1))
-    placed = jnp.zeros((rows, lanes), jnp.float32)
-    for which, column in enumerate(columns):
-        placed = jnp.where(at + which * rows == lane, column, placed)
-    return jnp.sum(placed, 0, keepdims=True)
-
-
 def three_parts(x):
     high = x.astype(jnp.bfloat16).astype(jnp.float32)
     mid = (x - high).astype(jnp.bfloat16).astype(jnp.float32)
@@ -139,19 +130,15 @@
     parts_out,
     parts,
     feats,
+    stacks,
     tiles,
-    corrs,
-    sums,
+    fields,
     ends,
     load_sem,
     part_send,
     part_recv,
     feat_send,
     feat_recv,
-    corr_send,
-    corr_recv,
-    sum_send,
-    sum_recv,
     end_send,
     end_recv,
 ):
@@ -235,8 +222,6 @@
     block_feat = whole[:n_feats]
     block_targ = whole[n_feats : n_feats + own_rhs]
     block_order = whole[n_feats + own_rhs : n_feats + own_rhs + 1]
-    feats[row] = block_feat
-
     def row_copy(buffer, send_sem, recv_sem, k, slot):
         return pltpu.make_async_remote_copy(
             src_ref=buffer.at[slot],
@@ -253,33 +238,70 @@
     def arrive(*copy):
         each(n_rows, lambda k: row_copy(*copy, k, row_peer(n_rows - k)).wait_recv())
 
-    feat_args = (feats, feat_send, feat_recv)
-    corr_args = [(corrs.at[t], corr_send.at[t], corr_recv.at[t]) for t in range(OUTER)]
-    sum_args = [(sums.at[t], sum_send.at[t], sum_recv.at[t]) for t in range(OUTER)]
-
-    spread(*feat_args)
-
     place = lax.broadcasted_iota(jnp.int32, (block, block), 0).astype(jnp.float32)
     picked = jnp.where(place == block_order, 1.0, 0.0).astype(jnp.bfloat16)
     three = jnp.concatenate(three_parts(block_targ), axis=0).astype(jnp.bfloat16)
     three = jnp.dot(three, picked, preferred_element_type=jnp.float32)
     residual = (three[:own_rhs] + three[own_rhs : 2 * own_rhs]) + three[2 * own_rhs :]
 
-    high, mid, low = three_parts(block_feat)
-    own_stack = jnp.transpose(jnp.concatenate([high, high, mid, mid, high, low], axis=0))
-    own_stack = own_stack.astype(jnp.bfloat16)
-    own_norm = jnp.transpose(
-        jnp.broadcast_to(jnp.sum(block_feat * block_feat, 0, keepdims=True), (8, block))
-    )[:, :1]
-
-    def tile_of(feat):
-        norm = jnp.sum(feat * feat, 0, keepdims=True)
-        high, mid, low = three_parts(feat)
-        stack = jnp.concatenate([high, mid, high, mid, low, high], axis=0).astype(jnp.bfloat16)
-        inner_prod = jnp.dot(own_stack, stack, preferred_element_type=jnp.float32)
-        return jnp.exp(-0.5 * (own_norm + norm - 2.0 * inner_prod)).astype(jnp.bfloat16)
-
-    block_tile = tile_of(block_feat)
+    everything = (feats, feat_send, feat_recv)
+    feats[row] = jnp.concatenate([block_feat, residual], axis=0)
+    spread(*everything)
+    arrive(*everything)
+
+    spare = lax.broadcasted_iota(jnp.int32, (16, block), 0)
+    log2e = 1.4426950408889634
+
+    def stack_of(feat, left):
+        high, mid, low = three_parts(feat * log2e if left else feat)
+        norm = three_parts((-0.5 * log2e) * jnp.sum(feat * feat, 0, keepdims=True))
+        first = 0 if left else 3
+        tail = jnp.where(spare < 6, 1.0, 0.0)
+        for which, part in enumerate(norm):
+            tail = jnp.where(spare == first + which, part, tail)
+        if left:
+            return jnp.concatenate([high, high, mid, mid, high, low, tail], axis=0)
+        return jnp.concatenate([high, mid, high, mid, low, high, tail], axis=0)
+
+    right = jnp.concatenate(
+        [stack_of(feats[b, :n_feats, :], False).astype(jnp.bfloat16) for b in range(n_rows)], axis=1
+    )
+    stacks[...] = right
+    points = n_rows * block
+    span = math.gcd(points, 4 * block)
+
+    def fill(b, carry):
+        left = jnp.transpose(stack_of(feats[b, :n_feats, :], True)).astype(jnp.bfloat16)
+        rows = pl.ds(pl.multiple_of(b * block, block), block)
+        for first in range(0, points, span):
+            power = jnp.dot(
+                left, stacks[:, first : first + span], preferred_element_type=jnp.float32
+            )
+            tiles[rows, first : first + span] = jnp.exp2(power).astype(jnp.bfloat16)
+        return carry
+
+    lax.fori_loop(0, n_rows, fill, 0)
+
+    noise_all = jnp.concatenate([noise_col] * n_rows, axis=0)
+
+    def block_images(packed):
+        return jnp.concatenate(
+            [
+                jnp.dot(
+                    packed[b * own_rhs : (b + 1) * own_rhs],
+                    tiles[b * block : (b + 1) * block, b * block : (b + 1) * block],
+                    preferred_element_type=jnp.float32,
+                )
+                for b in range(n_rows)
+            ],
+            axis=0,
+        )
+
+    def over_blocks(field):
+        summed = field[:own_rhs]
+        for b in range(1, n_rows):
+            summed = summed + field[b * own_rhs : (b + 1) * own_rhs]
+        return jnp.sum(summed, 1, keepdims=True)
 
     def solve(residual):
         remains = residual
@@ -287,12 +309,7 @@
         direction = remains
         correction = jnp.zeros_like(remains)
         for inner_turn in range(INNER):
-            image = (
-                jnp.dot(
-                    direction.astype(jnp.bfloat16), block_tile, preferred_element_type=jnp.float32
-                )
-                + noise_col * direction
-            )
+            image = block_images(direction.astype(jnp.bfloat16)) + noise_all * direction
             step_len = res_norm / jnp.sum(direction * image, 1, keepdims=True)
             correction = correction + step_len * direction
             if inner_turn + 1 < INNER:
@@ -302,29 +319,27 @@
                 res_norm = new_norm
         return correction
 
+    residual = jnp.concatenate([feats[b, n_feats:, :] for b in range(n_rows)], axis=0)
     solved = jnp.zeros_like(residual)
     for turn in range(OUTER):
         correction = solve(residual)
-        corrs[turn, row] = correction.astype(jnp.bfloat16)
-        spread(*corr_args[turn])
-        if turn == 0:
-            arrive(*feat_args)
-            for b in range(n_rows):
-                tiles[:, b * block : (b + 1) * block] = tile_of(feats[b])
-        arrive(*corr_args[turn])
-        everyone = jnp.concatenate([corrs[turn, b] for b in range(n_rows)], axis=1)
-        applied = noise_col * correction + lax.dot_general(
-            everyone, tiles[...], (((1,), (1,)), ((), ())), preferred_element_type=jnp.float32
-        )
-        cross = jnp.sum(residual * applied, 1, keepdims=True)
-        energy = jnp.sum(applied * applied, 1, keepdims=True)
-        sums[turn, row] = to_row((cross, energy), sums.shape[-1])
-        spread(*sum_args[turn])
-        arrive(*sum_args[turn])
-        total = jnp.sum(sums[turn], 0)
-        damping = to_column(total, own_rhs) / (to_column(total, own_rhs, own_rhs) + 1e-06)
+        packed = correction.astype(jnp.bfloat16)
+        packed = jnp.concatenate(
+            [packed[b * own_rhs : (b + 1) * own_rhs] for b in range(n_rows)], axis=1
+        )
+        full = jnp.dot(packed, tiles[...], preferred_element_type=jnp.float32)
+        applied = noise_all * correction + jnp.concatenate(
+            [full[:, b * block : (b + 1) * block] for b in range(n_rows)], axis=0
+        )
+        damping = over_blocks(residual * applied) / (over_blocks(applied * applied) + 1e-06)
+        damping = jnp.concatenate([damping] * n_rows, axis=0)
         solved = solved + damping * correction
         residual = residual - damping * applied
+    fields[0] = solved
+    fields[1] = residual
+    own_rows = pl.ds(pl.multiple_of(row * own_rhs, own_rhs), own_rhs)
+    solved = fields[0, own_rows, :]
+    residual = fields[1, own_rows, :]
 
     def end_copy(k, slot):
         return pltpu.make_async_remote_copy(
@@ -341,8 +356,7 @@
     each(n_cols, lambda k: end_copy(k, col).start())
 
     each(n_cols, lambda k: part_copy(k, col_peer(k), col).wait_send())
-    for copy in (feat_args, *corr_args, *sum_args):
-        each(n_rows, lambda k: row_copy(*copy, k, row).wait_send())
+    each(n_rows, lambda k: row_copy(*everything, k, row).wait_send())
 
     def own_points(field):
         points = field[:, :own_len]
@@ -374,25 +388,21 @@
             *(pltpu.VMEM(arg.shape, arg.dtype) for arg in args),
             pltpu.VMEM((n_cols, n_feats + own_rhs + 8, block), jnp.float32),
             pltpu.VMEM((n_cols, n_feats + own_rhs + 8, block), jnp.float32),
-            pltpu.VMEM((n_rows, n_feats, block), jnp.float32),
-            pltpu.VMEM((block, n_rows * block), jnp.bfloat16),
-            pltpu.VMEM((OUTER, n_rows, own_rhs, block), jnp.bfloat16),
-            pltpu.VMEM((OUTER, n_rows, 1, 128), jnp.float32),
+            pltpu.VMEM((n_rows, n_feats + own_rhs, block), jnp.float32),
+            pltpu.VMEM((6 * n_feats + 16, n_rows * block), jnp.bfloat16),
+            pltpu.VMEM((n_rows * block, n_rows * block), jnp.bfloat16),
+            pltpu.VMEM((2, n_rows * own_rhs, block), jnp.float32),
             pltpu.VMEM((n_cols, 2, own_rhs, block), jnp.float32),
             dma((len(args),)),
             dma((n_cols,)),
             dma((n_cols,)),
             dma((n_rows,)),
             dma((n_rows,)),
-            dma((OUTER, n_rows)),
-            dma((OUTER, n_rows)),
-            dma((OUTER, n_rows)),
-            dma((OUTER, n_rows)),
             dma((n_cols,)),
             dma((n_cols,)),
         ],
         compiler_params=pltpu.CompilerParams(
-            collective_id=0, has_side_effects=True, vmem_limit_bytes=32 * 1024 * 1024
+            collective_id=0, has_side_effects=True, vmem_limit_bytes=48 * 1024 * 1024
         ),
     )(*args)
 
@@ -402,9 +412,8 @@
     rhs = targets.shape[0]
     block = n_cols * own_len
     args = (features, targets, point_order, lengthscale, noise_var)
-    fits = 2 * n_rows * block * block <= 8 * 1024 * 1024
-    even = block % 128 == 0 and rhs % (16 * n_cols) == 0 and n_feats % 8 == 0
-    even = even and 2 * rhs // n_cols <= 128
+    fits = 2 * (n_rows * block) ** 2 <= 16 * 1024 * 1024
+    even = block % 128 == 0 and rhs % (16 * n_cols) == 0 and n_feats % 16 == 0
     if fits and even and n_rows > 1 and n_cols > 1:
         return body_small(n_rows, n_cols, *args)
     return body_large(*args)

time: 36.4 us -> 28.7 us (0.79)
  the two profiles are of different devices: /device:TPU:0 before, /device:TPU:15 now
where the time goes in v3:
time: 28.7 us; the launch traced here: 28.4 us
  Pallas kernels  24.4 us (85%)
  local copies, waits for them, and re-layouts  3.29 us (11%)
  between operations  0.67 us (2%)
    pallas_call x1, Pallas kernels, body_small(): pl.pallas_call(functools.partial(fused, n_rows, n_cols), out_shape=(out,...  24.4 us
    unnamed x12, local copies, waits for them, and re-layouts  3.29 us

profile of v3, /device:TPU:15, one launch (start us, length us, event | category | flops | bytes accessed | tf_op | source)
XLA Modules:
  0.0 28.4 jit_solution(7532506031248986898)
XLA Ops:
  0.6 0.0 copy-start.2
  0.6 0.0 copy-start.3
  0.7 0.0 copy-start.4
  0.7 0.6 %copy-done.2 = s32[64]{0:T(128)S(1)} copy-done((s32[64]{0:T(128)S(1)}, s32[64]{0:T(128)}, u32[]{:S(2)}) %copy-start.2) | copy-done | bytes 280
  1.3 0.0 copy-done.3
  1.3 0.0 copy-done.4
  1.3 0.0 copy-start
  1.3 0.7 %copy-done = f32[32,64]{1,0:T(8,128)S(1)} copy-done((f32[32,64]{1,0:T(8,128)S(1)}, f32[32,64]{1,0:T(8,128)}, u32[]{:S(2)}) %copy-start) | copy-done | bytes 8216
  2.0 0.0 copy-start.1
  2.0 0.7 %copy-done.1 = f32[16,64]{1,0:T(8,128)S(1)} copy-done((f32[16,64]{1,0:T(8,128)S(1)}, f32[16,64]{1,0:T(8,128)}, u32[]{:S(2)}) %copy-start.1) | copy-done | bytes 4120
  2.7 24.4 %shard_map.68 = (f32[32,64]{1,0:T(8,128)S(1)}, f32[32,64]{1,0:T(8,128)S(1)}) custom-call(f32[16,64]{1,0:T(8,128)S(1)} %copy-done.1, f32[32,64]{1,0:T(8,128)S(1)} %copy-done, s32[1,64]{1,0:T(1,128)S(1)} %bitcast.3, f32[1,16]{1,0:T(1,128)S(1)} %bitcast.4, f32[1,32]{1,0:T(1,128)S(1)} %bitcast.5), custom_call_target="tpu_custom_call" | custom-call | tf_op jit(solution)/shard_map/pallas_call | solution.py:382
  27.2 0.6 %copy.9 = f32[32,64]{1,0:T(8,128)} copy(f32[32,64]{1,0:T(8,128)S(1)} %get-tuple-element.4) | data formatting | bytes 16384
  27.8 0.6 %copy.10 = f32[32,64]{1,0:T(8,128)} copy(f32[32,64]{1,0:T(8,128)S(1)} %get-tuple-element.5) | data formatting | bytes 16384
Async XLA Ops:
  0.6 0.7 %copy-start.2 = (s32[64]{0:T(128)S(1)}, s32[64]{0:T(128)}, u32[]{:S(2)}) copy-start(s32[64]{0:T(128)} %param.7) | copy-start | bytes 772
  0.6 0.7 %copy-start.3 = (f32[16]{0:T(128)S(1)}, f32[16]{0:T(128)}, u32[]{:S(2)}) copy-start(f32[16]{0:T(128)} %param.8) | copy-start | bytes 196
  0.7 0.7 %copy-start.4 = (f32[32]{0:T(128)S(1)}, f32[32]{0:T(128)}, u32[]{:S(2)}) copy-start(f32[32]{0:T(128)} %param.9) | copy-start | bytes 388
  1.3 0.7 %copy-start = (f32[32,64]{1,0:T(8,128)S(1)}, f32[32,64]{1,0:T(8,128)}, u32[]{:S(2)}) copy-start(f32[32,64]{1,0:T(8,128)} %targ_hbm.1) | copy-start | bytes 24580
  2.0 0.7 %copy-start.1 = (f32[16,64]{1,0:T(8,128)S(1)}, f32[16,64]{1,0:T(8,128)}, u32[]{:S(2)}) copy-start(f32[16,64]{1,0:T(8,128)} %feat_hbm.1) | copy-start | bytes 12292

commit v4 on v3

--- a/solution.py
+++ b/solution.py
@@ -130,6 +130,7 @@
     parts_out,
     parts,
     feats,
+    resids,
     stacks,
     tiles,
     fields,
@@ -139,6 +140,8 @@
     part_recv,
     feat_send,
     feat_recv,
+    resid_send,
+    resid_recv,
     end_send,
     end_recv,
 ):
@@ -238,16 +241,20 @@
     def arrive(*copy):
         each(n_rows, lambda k: row_copy(*copy, k, row_peer(n_rows - k)).wait_recv())
 
+    feat_args = (feats, feat_send, feat_recv)
+    feats[row] = block_feat
+    spread(*feat_args)
+
     place = lax.broadcasted_iota(jnp.int32, (block, block), 0).astype(jnp.float32)
     picked = jnp.where(place == block_order, 1.0, 0.0).astype(jnp.bfloat16)
     three = jnp.concatenate(three_parts(block_targ), axis=0).astype(jnp.bfloat16)
     three = jnp.dot(three, picked, preferred_element_type=jnp.float32)
     residual = (three[:own_rhs] + three[own_rhs : 2 * own_rhs]) + three[2 * own_rhs :]
 
-    everything = (feats, feat_send, feat_recv)
-    feats[row] = jnp.concatenate([block_feat, residual], axis=0)
-    spread(*everything)
-    arrive(*everything)
+    resid_args = (resids, resid_send, resid_recv)
+    resids[row] = residual
+    spread(*resid_args)
+    arrive(*feat_args)
 
     spare = lax.broadcasted_iota(jnp.int32, (16, block), 0)
     log2e = 1.4426950408889634
@@ -264,14 +271,14 @@
         return jnp.concatenate([high, mid, high, mid, low, high, tail], axis=0)
 
     right = jnp.concatenate(
-        [stack_of(feats[b, :n_feats, :], False).astype(jnp.bfloat16) for b in range(n_rows)], axis=1
+        [stack_of(feats[b], False).astype(jnp.bfloat16) for b in range(n_rows)], axis=1
     )
     stacks[...] = right
     points = n_rows * block
     span = math.gcd(points, 4 * block)
 
     def fill(b, carry):
-        left = jnp.transpose(stack_of(feats[b, :n_feats, :], True)).astype(jnp.bfloat16)
+        left = jnp.transpose(stack_of(feats[b], True)).astype(jnp.bfloat16)
         rows = pl.ds(pl.multiple_of(b * block, block), block)
         for first in range(0, points, span):
             power = jnp.dot(
@@ -319,7 +326,8 @@
                 res_norm = new_norm
         return correction
 
-    residual = jnp.concatenate([feats[b, n_feats:, :] for b in range(n_rows)], axis=0)
+    arrive(*resid_args)
+    residual = jnp.concatenate([resids[b] for b in range(n_rows)], axis=0)
     solved = jnp.zeros_like(residual)
     for turn in range(OUTER):
         correction = solve(residual)
@@ -356,7 +364,8 @@
     each(n_cols, lambda k: end_copy(k, col).start())
 
     each(n_cols, lambda k: part_copy(k, col_peer(k), col).wait_send())
-    each(n_rows, lambda k: row_copy(*everything, k, row).wait_send())
+    for copy in (feat_args, resid_args):
+        each(n_rows, lambda k: row_copy(*copy, k, row).wait_send())
 
     def own_points(field):
         points = field[:, :own_len]
@@ -388,7 +397,8 @@
             *(pltpu.VMEM(arg.shape, arg.dtype) for arg in args),
             pltpu.VMEM((n_cols, n_feats + own_rhs + 8, block), jnp.float32),
             pltpu.VMEM((n_cols, n_feats + own_rhs + 8, block), jnp.float32),
-            pltpu.VMEM((n_rows, n_feats + own_rhs, block), jnp.float32),
+            pltpu.VMEM((n_rows, n_feats, block), jnp.float32),
+            pltpu.VMEM((n_rows, own_rhs, block), jnp.float32),
             pltpu.VMEM((6 * n_feats + 16, n_rows * block), jnp.bfloat16),
             pltpu.VMEM((n_rows * block, n_rows * block), jnp.bfloat16),
             pltpu.VMEM((2, n_rows * own_rhs, block), jnp.float32),
@@ -396,6 +406,8 @@
             dma((len(args),)),
             dma((n_cols,)),
             dma((n_cols,)),
+            dma((n_rows,)),
+            dma((n_rows,)),
             dma((n_rows,)),
             dma((n_rows,)),
             dma((n_cols,)),

time: 28.7 us -> 27.6 us (0.962)
  the two profiles are of different devices: /device:TPU:15 before, /device:TPU:13 now
where the time goes in v4:
time: 27.6 us; the launch traced here: 27.3 us
  Pallas kernels  23.3 us (84%)
  local copies, waits for them, and re-layouts  3.29 us (12%)
  between operations  0.67 us (2%)
    pallas_call x1, Pallas kernels, body_small(): pl.pallas_call(functools.partial(fused, n_rows, n_cols), out_shape=(out,...  23.3 us
    unnamed x12, local copies, waits for them, and re-layouts  3.29 us

profile of v4, /device:TPU:13, one launch (start us, length us, event | category | flops | bytes accessed | tf_op | source)
XLA Modules:
  0.0 27.3 jit_solution(12489094889799786491)
XLA Ops:
  0.6 0.0 copy-start.2
  0.6 0.0 copy-start.3
  0.7 0.0 copy-start.4
  0.7 0.6 %copy-done.2 = s32[64]{0:T(128)S(1)} copy-done((s32[64]{0:T(128)S(1)}, s32[64]{0:T(128)}, u32[]{:S(2)}) %copy-start.2) | copy-done | bytes 280
  1.3 0.0 copy-done.3
  1.3 0.0 copy-done.4
  1.3 0.0 copy-start
  1.3 0.7 %copy-done = f32[32,64]{1,0:T(8,128)S(1)} copy-done((f32[32,64]{1,0:T(8,128)S(1)}, f32[32,64]{1,0:T(8,128)}, u32[]{:S(2)}) %copy-start) | copy-done | bytes 8216
  2.0 0.0 copy-start.1
  2.0 0.7 %copy-done.1 = f32[16,64]{1,0:T(8,128)S(1)} copy-done((f32[16,64]{1,0:T(8,128)S(1)}, f32[16,64]{1,0:T(8,128)}, u32[]{:S(2)}) %copy-start.1) | copy-done | bytes 4120
  2.7 23.3 %shard_map.68 = (f32[32,64]{1,0:T(8,128)S(1)}, f32[32,64]{1,0:T(8,128)S(1)}) custom-call(f32[16,64]{1,0:T(8,128)S(1)} %copy-done.1, f32[32,64]{1,0:T(8,128)S(1)} %copy-done, s32[1,64]{1,0:T(1,128)S(1)} %bitcast.3, f32[1,16]{1,0:T(1,128)S(1)} %bitcast.4, f32[1,32]{1,0:T(1,128)S(1)} %bitcast.5), custom_call_target="tpu_custom_call" | custom-call | tf_op jit(solution)/shard_map/pallas_call | solution.py:391
  26.0 0.6 %copy.9 = f32[32,64]{1,0:T(8,128)} copy(f32[32,64]{1,0:T(8,128)S(1)} %get-tuple-element.4) | data formatting | bytes 16384
  26.6 0.6 %copy.10 = f32[32,64]{1,0:T(8,128)} copy(f32[32,64]{1,0:T(8,128)S(1)} %get-tuple-element.5) | data formatting | bytes 16384
Async XLA Ops:
  0.6 0.7 %copy-start.2 = (s32[64]{0:T(128)S(1)}, s32[64]{0:T(128)}, u32[]{:S(2)}) copy-start(s32[64]{0:T(128)} %param.7) | copy-start | bytes 772
  0.6 0.7 %copy-start.3 = (f32[16]{0:T(128)S(1)}, f32[16]{0:T(128)}, u32[]{:S(2)}) copy-start(f32[16]{0:T(128)} %param.8) | copy-start | bytes 196
  0.7 0.7 %copy-start.4 = (f32[32]{0:T(128)S(1)}, f32[32]{0:T(128)}, u32[]{:S(2)}) copy-start(f32[32]{0:T(128)} %param.9) | copy-start | bytes 388
  1.3 0.7 %copy-start = (f32[32,64]{1,0:T(8,128)S(1)}, f32[32,64]{1,0:T(8,128)}, u32[]{:S(2)}) copy-start(f32[32,64]{1,0:T(8,128)} %targ_hbm.1) | copy-start | bytes 24580
  2.0 0.7 %copy-start.1 = (f32[16,64]{1,0:T(8,128)S(1)}, f32[16,64]{1,0:T(8,128)}, u32[]{:S(2)}) copy-start(f32[16,64]{1,0:T(8,128)} %feat_hbm.1) | copy-start | bytes 12292
